TPU v7x, 256 devices: a whole 4x4x8 slice. The times are simulated.
256 devices in a mesh: gx: 4 (over y), gy: 8 (over z_lo, x), gz: 8 (over z_hi, core).
Axes of the slice: x: 4, y: 4, z: 8 (z_hi: 4, z_lo: 2; z = z_hi * 2 + z_lo), core: 2. Of those that a mesh axis runs over, the one named last changes fastest.
Arguments:
- saved_input: bfloat16 [1536, 12288], P('gx', ('gy', 'gz')), may hold values from -6 to 6
- weight: bfloat16 [12288, 24576], P('gy', ('gz', 'gx')), may hold values from -0.0546875 to 0.0546875
- out_grad: bfloat16 [1536, 24576], P('gx', ('gz', 'gy')), may hold values from -16 to 16
Outputs:
- input_grad: bfloat16 [1536, 12288], P('gx', ('gy', 'gz'))
- weight_grad: bfloat16 [12288, 24576], P('gy', ('gz', 'gx'))
All inputs are finite; a program needn't handle non-finite values.
Results may differ from a plain program's by a relative error of at most 0.022.
Values may be sent and summed in bfloat16 or wider, within the bound.
A program may use at most 128 MiB of HBM per device.

v0:
```python
import jax
import jax.numpy as jnp
from jax import lax
from jax.sharding import PartitionSpec as P


def gelu_slope(pre, grad):
    _, pullback = jax.vjp(lambda values: jax.nn.gelu(values, approximate=True), pre)
    return pullback(grad.astype(jnp.float32))[0]


def local(saved_input, weight, out_grad):
    inputs_whole = lax.all_gather(saved_input, "gz", axis=1, tiled=True)
    weights_whole = lax.all_gather(weight, "gx", axis=1, tiled=True)
    partial_value = jnp.dot(inputs_whole, weights_whole, preferred_element_type=jnp.float32)
    pre = lax.psum(partial_value.astype(jnp.bfloat16), "gy").astype(jnp.float32)
    grad_whole = lax.all_gather(out_grad, "gy", axis=1, tiled=True)
    pre_grad = gelu_slope(pre, grad_whole).astype(jnp.bfloat16)
    input_terms = lax.dot_general(
        pre_grad, weights_whole, (((1,), (1,)), ((), ())), preferred_element_type=jnp.float32
    )
    input_grad = lax.psum_scatter(
        input_terms.astype(jnp.bfloat16), "gz", scatter_dimension=1, tiled=True
    )
    weight_terms = lax.dot_general(
        inputs_whole, pre_grad, (((0,), (0,)), ((), ())), preferred_element_type=jnp.float32
    )
    weight_grad = lax.psum_scatter(
        weight_terms.astype(jnp.bfloat16), "gx", scatter_dimension=1, tiled=True
    )
    return (input_grad, weight_grad)


def solution(mesh):
    placed = (P("gx", ("gy", "gz")), P("gy", ("gz", "gx")), P("gx", ("gz", "gy")))
    return jax.shard_map(
        local,
        mesh=mesh,
        in_specs=placed,
        out_specs=(P("gx", ("gy", "gz")), P("gy", ("gz", "gx"))),
        check_vma=False,
    )
```

profile of v0, /device:TPU:1, one launch (start us, length us, event | category | flops | bytes accessed | tf_op | source)
XLA Modules:
  0.0 431.0 jit_solution(11693341544042525622)
XLA Ops:
  7.2 0.0 all-gather.6.cloned.1.call-start
  7.2 0.7 all-gather.6.cloned.1.call-update
  7.9 0.0 all-gather.8.cloned.1.call-start
  7.9 0.7 all-gather.8.cloned.1.call-update
  8.6 0.0 all-gather.4.cloned.1.call-start
  8.7 0.7 all-gather.4.cloned.1.call-update
  9.4 0.0 all-reduce.2.cloned.1.call-start
  9.4 35.3 %all-gather.6.cloned.1.call-done = bf16[384,1536]{0,1:T(8,128)(2,1)} async-done(((bf16[384,192]{0,1:T(8,128)(2,1)}), bf16[384,1536]{0,1:T(8,128)(2,1)}) %all-gather.6.cloned.1.call-update) | async-done | bytes 1179664 | tf_op jit(solution)/shard_map/all_gather | solution.py:13
  44.7 0.0 copy-start.1
  44.7 94.8 %all-gather.8.cloned.1.call-done = bf16[1536,3072]{1,0:T(8,128)(2,1)} async-done(((bf16[1536,768]{1,0:T(8,128)(2,1)}), bf16[1536,3072]{1,0:T(8,128)(2,1)}) %all-gather.8.cloned.1.call-update) | async-done | bytes 9437200 | tf_op jit(solution)/shard_map/all_gather | solution.py:14
  139.5 9.4 %convolution_convert_fusion.1 = bf16[384,3072]{1,0:T(8,128)(2,1)} fusion(bf16[384,1536]{0,1:T(8,128)(2,1)} %all-gather.6.cloned.1.call-done, bf16[1536,3072]{1,0:T(8,128)(2,1)} %all-gather.8.cloned.1.call-done), kind=kOutput, calls=%fused_computation.17 | convolution fusion | flops 3625058304 | bytes 12976128 | tf_op jit(solution)/shard_map/dot_general | solution.py:15
  148.8 0.0 all-reduce.2.cloned.1.call-update
  148.9 0.0 reduce-scatter.5.cloned.1.call-start
  148.9 34.0 %all-gather.4.cloned.1.call-done = bf16[384,3072]{1,0:T(8,128)(2,1)} async-done(((bf16[384,384]{1,0:T(8,128)(2,1)}), bf16[384,3072]{1,0:T(8,128)(2,1)}) %all-gather.4.cloned.1.call-update) | async-done | bytes 2359312 | tf_op jit(solution)/shard_map/all_gather | solution.py:17
  182.9 93.1 %all-reduce.2.cloned.1.call-done = bf16[384,3072]{1,0:T(8,128)(2,1)} async-done(((bf16[384,3072]{1,0:T(8,128)(2,1)}), bf16[384,3072]{1,0:T(8,128)(2,1)}) %all-reduce.2.cloned.1.call-update) | async-done | bytes 2359312 | tf_op jit(solution)/shard_map/psum | solution.py:16
  276.0 0.0 copy-done.1
  276.0 12.0 %fusion = bf16[1536,3072]{0,1:T(8,128)(2,1)} fusion(bf16[384,1536]{0,1:T(8,128)(2,1)S(1)} %copy-done.1, bf16[384,3072]{1,0:T(8,128)(2,1)} %all-gather.4.cloned.1.call-done, bf16[384,3072]{1,0:T(8,128)(2,1)} %all-reduce.2.cloned.1.call-done), kind=kOutput, calls=%fused_computation.1 | convolution fusion | flops 3654549504 | bytes 15335424 | tf_op jit(solution)/shard_map/dot_general | solution.py:25
  288.0 0.0 copy-start
  288.0 0.0 reduce-scatter.5.cloned.1.call-update
  288.0 0.2 reduce-scatter.3.cloned.1.call-start
  288.2 1.4 copy-done
  289.7 10.9 %convolution_convert_fusion.2 = bf16[384,1536]{0,1:T(8,128)(2,1)} fusion(bf16[1536,3072]{1,0:T(8,128)(2,1)} %all-gather.8.cloned.1.call-done, bf16[384,3072]{1,0:T(8,128)(2,1)S(1)} %copy-done, bf16[384,3072]{1,0:T(8,128)(2,1)} %all-reduce.2.cloned.1.call-done), kind=kOutput, calls=%fused_computation.18 | convolution fusion | flops 3650420736 | bytes 15335424 | tf_op jit(solution)/shard_map/dot_general | solution.py:19
  300.6 0.0 reduce-scatter.3.cloned.1.call-update
  300.6 82.7 %reduce-scatter.5.cloned.1.call-done = bf16[1536,768]{0,1:T(8,128)(2,1)} async-done(((bf16[1536,3072]{0,1:T(8,128)(2,1)}), bf16[1536,768]{0,1:T(8,128)(2,1)}) %reduce-scatter.5.cloned.1.call-update) | async-done | bytes 2359312 | tf_op jit(solution)/shard_map/reduce_scatter | solution.py:28
  383.3 4.3 copy.5
  387.5 36.6 %reduce-scatter.3.cloned.1.call-done = bf16[384,192]{0,1:T(8,128)(2,1)} async-done(((bf16[384,1536]{0,1:T(8,128)(2,1)}), bf16[384,192]{0,1:T(8,128)(2,1)}) %reduce-scatter.3.cloned.1.call-update) | async-done | bytes 147472 | tf_op jit(solution)/shard_map/reduce_scatter | solution.py:22
Async XLA Ops:
  7.2 37.5 %all-gather.6.cloned.1.call-start = ((), (), s32[]{:S(2)}) async-start(), calls=%async_computation.3 | async-start | bytes 1327104 | tf_op jit(solution)/shard_map/all_gather | solution.py:13
  7.9 131.6 %all-gather.8.cloned.1.call-start = ((), (), s32[]{:S(2)}) async-start(), calls=%async_computation.4 | async-start | bytes 11796480 | tf_op jit(solution)/shard_map/all_gather | solution.py:14
  8.6 174.2 %all-gather.4.cloned.1.call-start = ((), (), s32[]{:S(2)}) async-start(), calls=%async_computation.2 | async-start | bytes 2654208 | tf_op jit(solution)/shard_map/all_gather | solution.py:17
  9.4 266.6 %all-reduce.2.cloned.1.call-start = ((), (), s32[]{:S(2)}) async-start(), calls=%async_computation.5 | async-start | bytes 4718592 | tf_op jit(solution)/shard_map/psum | solution.py:16
  44.7 231.3 %copy-start.1 = (bf16[384,1536]{0,1:T(8,128)(2,1)S(1)}, bf16[384,1536]{0,1:T(8,128)(2,1)}, u32[]{:S(2)}) copy-start(bf16[384,1536]{0,1:T(8,128)(2,1)} %all-gather.6.cloned.1.call-done) | copy-start | bytes 3538948
  148.9 234.4 %reduce-scatter.5.cloned.1.call-start = ((), (), s32[]{:S(2)}) async-start(), calls=%async_computation.7 | async-start | bytes 11796480 | tf_op jit(solution)/shard_map/reduce_scatter | solution.py:28
  288.0 1.7 copy-start
  288.0 136.1 %reduce-scatter.3.cloned.1.call-start = ((), (), s32[]{:S(2)}) async-start(), calls=%async_computation.6 | async-start | bytes 1327104 | tf_op jit(solution)/shard_map/reduce_scatter | solution.py:22
Sparse Core Ops, SparseCore 0:
  9.8 34.8 all-gather.5
  46.5 92.9 all-gather.7
  141.3 41.5 all-gather.3
  186.0 89.9 all-reduce.1
  288.1 95.0 reduce-scatter.4
  386.2 37.8 reduce-scatter.2
where the time goes:
time: 432 us; the launch traced here: 431 us
  waiting for transfers between devices  379 us (88%)
  matrix products  32.3 us (7%)
  between operations  14.1 us (3%)
  local copies, waits for them, and re-layouts  5.68 us (1%)
    all_gather x1, waiting for transfers between devices, local(): weights_whole = lax.all_gather(weight, 'gx', axis=1, tiled=True)  94.8 us
    psum x1, waiting for transfers between devices, local(): pre = lax.psum(partial_value.astype(jnp.bfloat16), 'gy').astype(jnp.float32)  93.1 us
    reduce_scatter x1, waiting for transfers between devices, local(): lax.psum_scatter(weight_terms.astype(jnp.bfloat16), 'gx', scatter_dimensi...  82.7 us
    reduce_scatter x1, waiting for transfers between devices, local(): lax.psum_scatter(input_terms.astype(jnp.bfloat16), 'gz', scatter_dimensio...  36.6 us
    all_gather x1, waiting for transfers between devices, local(): inputs_whole = lax.all_gather(saved_input, 'gz', axis=1, tiled=True)  35.3 us
    all_gather x1, waiting for transfers between devices, local(): grad_whole = lax.all_gather(out_grad, 'gy', axis=1, tiled=True)  34 us
    dot_general x1, matrix products, local(): lax.dot_general(inputs_whole, pre_grad, (((0,), (0,)), ((), ())), preferr...  12 us
    dot_general x1, matrix products, local(): lax.dot_general(pre_grad, weights_whole, (((1,), (1,)), ((), ())), prefer...  10.9 us
  transfers between devices with their start and end apart: 6, of which 6 were waited for; matrix products, arithmetic and copies ran while one was open for 6% of the time, Pallas kernels for 0%

commit v1 on v0

v1 whole, which is shorter than its diff:
```python
import jax
import jax.numpy as jnp
from jax import lax
from jax.sharding import PartitionSpec as P


def gelu_slope(pre, grad):
    _, pullback = jax.vjp(lambda values: jax.nn.gelu(values, approximate=True), pre)
    return pullback(grad.astype(jnp.float32))[0]


def local(saved_input, weight, out_grad):
    feats = lax.all_gather(saved_input, "gz", axis=1, tiled=True)
    inputs = lax.all_gather(feats, "gx", axis=0, tiled=True)
    partial_value = jnp.dot(inputs, weight, preferred_element_type=jnp.float32).astype(jnp.bfloat16)
    pieces = partial_value.reshape(4, 384, 2, 384).transpose(0, 2, 1, 3).reshape(8 * 384, 384)
    pre = lax.psum_scatter(pieces, "gy", scatter_dimension=0, tiled=True).astype(jnp.float32)
    perm = [(t * 8 + 2 * a + h, a * 8 + 2 * t + h) for t in range(4) for a in range(4) for h in range(2)]
    grad = lax.ppermute(out_grad, ("gx", "gy"), perm)
    piece_grad = gelu_slope(pre, grad).astype(jnp.bfloat16)
    gathered = lax.all_gather(piece_grad, "gy", axis=0, tiled=True)
    pre_grad = gathered.reshape(4, 2, 384, 384).transpose(0, 2, 1, 3).reshape(1536, 768)
    input_terms = lax.dot_general(
        pre_grad, weight, (((1,), (1,)), ((), ())), preferred_element_type=jnp.float32
    ).astype(jnp.bfloat16)
    by_token = lax.psum_scatter(input_terms, "gx", scatter_dimension=0, tiled=True)
    input_grad = lax.psum_scatter(by_token, "gz", scatter_dimension=1, tiled=True)
    weight_grad = lax.dot_general(
        inputs, pre_grad, (((0,), (0,)), ((), ())), preferred_element_type=jnp.float32
    ).astype(jnp.bfloat16)
    return (input_grad, weight_grad)


def solution(mesh):
    placed = (P("gx", ("gy", "gz")), P("gy", ("gz", "gx")), P("gx", ("gz", "gy")))
    return jax.shard_map(
        local,
        mesh=mesh,
        in_specs=placed,
        out_specs=(P("gx", ("gy", "gz")), P("gy", ("gz", "gx"))),
        check_vma=False,
    )
```

time: 432 us -> 326 us (0.75)
  waiting for transfers between devices: 379 us -> 262 us
  local copies, waits for them, and re-layouts: 5.68 us -> 22.7 us
  matrix products: 32.3 us -> 21.6 us
    psum x1 -> x0, waiting for transfers between devices: 93.1 us -> none  [local(): pre = lax.psum(partial_value.astype(jnp.bfloat16), 'gy').astype(jnp.float32)]
    all_gather x3, waiting for transfers between devices: 164 us -> 135 us  [the longest x1 55.4 us: local(): inputs = lax.all_gather(feats, 'gx', axis=0, tiled=True)]
    unnamed x6 -> x7, waiting for transfers between devices: 2.11 us -> 26.2 us
    reduce_scatter x2, waiting for transfers between devices: 119 us -> 101 us  [the longest x1 57.4 us: local(): lax.psum_scatter(input_terms, 'gx', scatter_dimension=0, tiled=True)]
    dot_general x3, matrix products: 32.3 us -> 21.6 us  [the longest x1 8.36 us: local(): lax.dot_general(inputs, pre_grad, (((0,), (0,)), ((), ())), preferred_ele...]
    reshape x0 -> x2, local copies, waits for them, and re-layouts: none -> 9.86 us  [the longest x1 5.77 us: local(): partial_value.reshape(4, 384, 2, 384).transpose(0, 2, 1, 3)]
    unnamed x5 -> x9, local copies, waits for them, and re-layouts: 5.68 us -> 9.48 us
  transfers between devices with their start and end apart: 6 -> 7, of which waited for: 6 -> 6; matrix products, arithmetic and copies ran while one was open for 6% -> 4% of each run, Pallas kernels for 0% -> 0%
where the time goes in v1:
time: 326 us; the launch traced here: 324 us
  waiting for transfers between devices  262 us (80%)
  local copies, waits for them, and re-layouts  22.7 us (7%)
  matrix products  21.6 us (7%)
  between operations  14.2 us (4%)
    reduce_scatter x1, waiting for transfers between devices, local(): lax.psum_scatter(input_terms, 'gx', scatter_dimension=0, tiled=True)  57.4 us
    all_gather x1, waiting for transfers between devices, local(): inputs = lax.all_gather(feats, 'gx', axis=0, tiled=True)  55.4 us
    reduce_scatter x1, waiting for transfers between devices, local(): lax.psum_scatter(pieces, 'gy', scatter_dimension=0, tiled=True)  44 us
    all_gather x1, waiting for transfers between devices, local(): gathered = lax.all_gather(piece_grad, 'gy', axis=0, tiled=True)  42.4 us
    all_gather x1, waiting for transfers between devices, local(): feats = lax.all_gather(saved_input, 'gz', axis=1, tiled=True)  36.8 us
    unnamed x7, waiting for transfers between devices  26.2 us
    unnamed x9, local copies, waits for them, and re-layouts  9.48 us
    dot_general x1, matrix products, local(): lax.dot_general(inputs, pre_grad, (((0,), (0,)), ((), ())), preferred_ele...  8.36 us
  transfers between devices with their start and end apart: 7, of which 6 were waited for; matrix products, arithmetic and copies ran while one was open for 4% of the time, Pallas kernels for 0%

profile of v1, /device:TPU:1, one launch (start us, length us, event | category | flops | bytes accessed | tf_op | source)
XLA Modules:
  0.0 323.8 jit_solution(7194313026958584015)
XLA Ops:
  7.2 0.0 copy-start
  7.2 0.0 all-gather.4.cloned.1.call-start
  7.2 0.7 all-gather.4.cloned.1.call-update
  7.9 0.0 all-gather.6.cloned.1.call-start
  8.0 36.8 %all-gather.4.cloned.1.call-done = bf16[384,1536]{0,1:T(8,128)(2,1)} async-done(((bf16[384,192]{0,1:T(8,128)(2,1)}), bf16[384,1536]{0,1:T(8,128)(2,1)}) %all-gather.4.cloned.1.call-update) | async-done | bytes 1179664 | tf_op jit(solution)/shard_map/all_gather | solution.py:13
  44.7 0.0 all-gather.6.cloned.1.call-update
  44.8 0.0 reduce-scatter.6.cloned.1.call-start
  44.8 55.4 %all-gather.6.cloned.1.call-done = bf16[1536,1536]{0,1:T(8,128)(2,1)} async-done(((bf16[384,1536]{0,1:T(8,128)(2,1)}), bf16[1536,1536]{0,1:T(8,128)(2,1)}) %all-gather.6.cloned.1.call-update) | async-done | bytes 4718608 | tf_op jit(solution)/shard_map/all_gather | solution.py:14
  100.2 0.0 copy-done
  100.2 7.5 %convolution_convert_fusion.2 = bf16[1536,768]{1,0:T(8,128)(2,1)} fusion(bf16[1536,1536]{0,1:T(8,128)(2,1)} %all-gather.6.cloned.1.call-done, bf16[1536,768]{1,0:T(8,128)(2,1)S(1)} %copy-done), kind=kOutput, calls=%fused_computation.2 | convolution fusion | flops 3625058304 | bytes 9437184 | tf_op jit(solution)/shard_map/dot_general | solution.py:15
  107.7 5.8 %reshape.16 = bf16[4,384,2,384]{3,2,1,0:T(2,128)(2,1)} reshape(bf16[1536,768]{1,0:T(8,128)(2,1)} %convolution_convert_fusion.2) | data formatting | bytes 4718592 | tf_op jit(solution)/shard_map/reshape | solution.py:16
  113.5 3.4 %copy.12 = bf16[4,2,384,384]{3,2,1,0:T(8,128)(2,1)} copy(bf16[4,2,384,384]{3,1,2,0:T(2,128)(2,1)} %bitcast.18) | data formatting | bytes 4718592 | tf_op jit(solution)/shard_map/transpose | solution.py:16
  116.9 0.0 copy-start.2
  116.9 0.0 reduce-scatter.6.cloned.1.call-update
  116.9 0.0 all-gather.8.cloned.1.call-start
  117.0 0.9 copy-done.2
  117.8 0.7 collective-permute-start
  118.5 0.0 collective-permute-done
  118.5 44.0 %reduce-scatter.6.cloned.1.call-done = bf16[384,384]{1,0:T(8,128)(2,1)} async-done(((bf16[3072,384]{1,0:T(8,128)(2,1)}), bf16[384,384]{1,0:T(8,128)(2,1)}) %reduce-scatter.6.cloned.1.call-update) | async-done | bytes 294928 | tf_op jit(solution)/shard_map/reduce_scatter | solution.py:17
  162.6 2.1 fusion.4
  164.7 0.0 all-gather.8.cloned.1.call-update
  164.7 0.0 reduce-scatter.8.cloned.1.call-start
  164.8 42.4 %all-gather.8.cloned.1.call-done = bf16[3072,384]{1,0:T(8,128)(2,1)} async-done(((bf16[384,384]{1,0:T(8,128)(2,1)}), bf16[3072,384]{1,0:T(8,128)(2,1)}) %all-gather.8.cloned.1.call-update) | async-done | bytes 2359312 | tf_op jit(solution)/shard_map/all_gather | solution.py:21
  207.1 4.1 %copy.13 = bf16[4,2,384,384]{3,1,2,0:T(2,128)(2,1)S(1)} copy(bf16[4,2,384,384]{3,2,1,0:T(8,128)(2,1)} %bitcast.23) | data formatting | bytes 4718592 | tf_op jit(solution)/shard_map/reshape | solution.py:22
  211.2 0.5 copy.18
  211.7 0.0 copy-start.1
  211.7 1.4 copy-done.1
  213.1 5.7 %convolution_convert_fusion = bf16[1536,1536]{1,0:T(8,128)(2,1)} fusion(bf16[1536,768]{1,0:T(8,128)(2,1)S(1)} %bitcast.21, bf16[1536,768]{1,0:T(8,128)(2,1)S(1)} %copy-done), kind=kOutput, calls=%fused_computation | convolution fusion | flops 3626237952 | bytes 9437184 | tf_op jit(solution)/shard_map/dot_general | solution.py:23
  218.8 0.0 reduce-scatter.8.cloned.1.call-update
  218.8 0.2 reduce-scatter.10.cloned.1.call-start
  219.0 57.4 %reduce-scatter.8.cloned.1.call-done = bf16[384,1536]{1,0:T(8,128)(2,1)} async-done(((bf16[1536,1536]{1,0:T(8,128)(2,1)}), bf16[384,1536]{1,0:T(8,128)(2,1)}) %reduce-scatter.8.cloned.1.call-update) | async-done | bytes 1179664 | tf_op jit(solution)/shard_map/reduce_scatter | solution.py:26
  276.5 2.4 copy.16
  278.9 0.0 reduce-scatter.10.cloned.1.call-update
  278.9 8.4 %fusion = bf16[1536,768]{0,1:T(8,128)(2,1)} fusion(bf16[1536,768]{1,0:T(8,128)(2,1)} %bitcast.22, bf16[1536,1536]{0,1:T(8,128)(2,1)} %all-gather.6.cloned.1.call-done), kind=kOutput, calls=%fused_computation.3 | convolution fusion | flops 3625058304 | bytes 9437184 | tf_op jit(solution)/shard_map/dot_general | solution.py:28
  287.3 4.3 %copy.15 = bf16[1536,768]{1,0:T(8,128)(2,1)} copy(bf16[1536,768]{0,1:T(8,128)(2,1)} %fusion) | data formatting | bytes 4718592
  291.5 25.4 %reduce-scatter.10.cloned.1.call-done = bf16[192,384]{1,0:T(8,128)(2,1)} async-done(((bf16[1536,384]{1,0:T(8,128)(2,1)}), bf16[192,384]{1,0:T(8,128)(2,1)}) %reduce-scatter.10.cloned.1.call-update) | async-done | bytes 147472
Async XLA Ops:
  7.2 93.0 %copy-start = (bf16[1536,768]{1,0:T(8,128)(2,1)S(1)}, bf16[1536,768]{1,0:T(8,128)(2,1)}, u32[]{:S(2)}) copy-start(bf16[1536,768]{1,0:T(8,128)(2,1)} %param.4) | copy-start | bytes 7077892
  7.2 37.5 %all-gather.4.cloned.1.call-start = ((), (), s32[]{:S(2)}) async-start(), calls=%async_computation.3 | async-start | bytes 1327104 | tf_op jit(solution)/shard_map/all_gather | solution.py:13
  7.9 92.3 %all-gather.6.cloned.1.call-start = ((), (), s32[]{:S(2)}) async-start(), calls=%async_computation.4 | async-start | bytes 5898240 | tf_op jit(solution)/shard_map/all_gather | solution.py:14
  44.8 117.8 %reduce-scatter.6.cloned.1.call-start = ((), (), s32[]{:S(2)}) async-start(), calls=%async_computation.5 | async-start | bytes 2654208 | tf_op jit(solution)/shard_map/reduce_scatter | solution.py:17
  116.9 1.0 copy-start.2
  116.9 90.2 %all-gather.8.cloned.1.call-start = ((), (), s32[]{:S(2)}) async-start(), calls=%async_computation.6 | async-start | bytes 2654208 | tf_op jit(solution)/shard_map/all_gather | solution.py:21
  117.8 0.7 collective-permute-start
  164.7 111.7 %reduce-scatter.8.cloned.1.call-start = ((), (), s32[]{:S(2)}) async-start(), calls=%async_computation.7 | async-start | bytes 5898240 | tf_op jit(solution)/shard_map/reduce_scatter | solution.py:26
  211.7 1.4 copy-start.1
  218.8 98.2 %reduce-scatter.10.cloned.1.call-start = ((), (), s32[]{:S(2)}) async-start(), calls=%async_computation.8 | async-start | bytes 1327104
Sparse Core Ops, SparseCore 0:
  9.8 34.8 all-gather.3
  46.6 53.5 all-gather.5
  117.0 45.5 reduce-scatter.5
  164.8 42.2 all-gather.7
  218.9 57.4 reduce-scatter.7
  279.4 37.5 reduce-scatter.9

commit v2 on v1

v2 whole, which is shorter than its diff:
```python
import jax
import jax.numpy as jnp
from jax import lax
from jax.experimental import pallas as pl
from jax.experimental.pallas import tpu as pltpu
from jax.sharding import PartitionSpec as P

MESH = pl.DeviceIdType.MESH
F32 = jnp.float32
BF16 = jnp.bfloat16
ROOT = 0.7978845608028654
CUBE = 0.044715
N_SEM = 160


def gelu_slope(pre, grad):
    square = pre * pre
    tanh = jnp.tanh(ROOT * (pre + CUBE * (pre * square)))
    slope = 0.5 * (1.0 + tanh) + (0.5 * ROOT) * pre * (1.0 - tanh * tanh) * (1.0 + 3.0 * CUBE * square)
    return grad * slope


def kernel(x_ref, w_hbm, g_ref, dx_out, dw_out,
           wv, wt, gt, gl, xt, pp, rz, s1, rx, pt, dx, rc, sy, ry, sz, rzz, dwv,
           ssem, rsem, lsem):
    y, gy, gz = lax.axis_index("gx"), lax.axis_index("gy"), lax.axis_index("gz")
    zl, x = gy // 4, gy % 4
    zh, c = gz // 2, gz % 2

    core = (y, gy, zh * 2 + (1 - c))
    zlp = (y, (1 - zl) * 4 + x, gz)

    def on_y(d):
        return ((y + d) % 4, gy, gz)

    def on_x(d):
        return (y, zl * 4 + (x + d) % 4, gz)

    def on_z(d):
        return (y, gy, ((zh + d) % 4) * 2 + c)

    g_dst = [(2 * zl + x // 2, z * 4 + 2 * (x % 2) + k, gz) for k in range(2) for z in range(2)]
    g_rows = [(2 * k + z) * 96 for k in range(2) for z in range(2)]
    g_src = [(t, (y // 2) * 4 + 2 * (y % 2) + x // 2, gz) for t in range(4)]
    own_g = jnp.logical_and(zl == y // 2, x == 2 * (y % 2) + x // 2)
    count = [0]
    sends = []

    def slot():
        count[0] += 1
        return count[0] - 1

    def send(src, dst, to, k):
        cp = pltpu.make_async_remote_copy(src, dst, ssem.at[k], rsem.at[k], device_id=to, device_id_type=MESH)
        cp.start()
        sends.append(cp)

    def arrived(dst, k):
        pltpu.make_async_remote_copy(dst, dst, ssem.at[k], rsem.at[k], device_id=core, device_id_type=MESH).wait_recv()

    w_copy = pltpu.make_async_copy(w_hbm, wv, lsem.at[0])
    w_copy.start()
    x_copy = pltpu.make_async_copy(x_ref, xt.at[0, zh, c], lsem.at[1])
    x_copy.start()

    barrier = pltpu.get_barrier_semaphore()
    partners = [core, zlp] + [on_y(d) for d in (1, 2, 3)] + [on_x(d) for d in (1, 2, 3)] + [on_z(d) for d in (1, 2, 3)]
    for p in partners:
        pl.semaphore_signal(barrier, inc=1, device_id=p, device_id_type=MESH)
    for t in range(4):
        @pl.when(jnp.logical_not(jnp.logical_and(own_g, y == t)))
        def _(t=t):
            pl.semaphore_signal(barrier, inc=1, device_id=g_src[t], device_id_type=MESH)
    pl.semaphore_wait(barrier, len(partners) + 4 - own_g.astype(jnp.int32))

    k_z = [None] + [slot() for _ in range(3)]
    k_c0 = [slot() for _ in range(4)]
    k_y = [[slot() for _ in range(4)] for _ in range(2)]
    k_cy = [[slot() for _ in range(4)] for _ in range(2)]
    k_f = [[slot() for _ in range(4)] for _ in range(2)]
    k_cf = [[slot() for _ in range(4)] for _ in range(2)]

    def zof(d):
        return (zh - d + 4) % 4

    for d in (2, 1, 3):
        send(x_ref, xt.at[0, zh, c], on_z(d), k_z[d])
    send(x_ref, xt.at[3, zh, c], on_y(1), k_y[0][0])
    send(x_ref, xt.at[1, zh, c], on_y(3), k_y[1][0])
    send(x_ref, xt.at[0, zh, c], core, k_c0[0])

    gt[...] = g_ref[...].T
    k_g = [slot() for _ in range(4)]
    g_sends = []
    for n in range(4):
        a, dgy, _ = g_dst[n]
        r = (y - a + 4) % 4
        here = jnp.logical_and(a == y, dgy == gy)
        src = gt.at[pl.ds(g_rows[n], 96)]
        cp = pltpu.make_async_remote_copy(src, gl.at[r], ssem.at[k_g[n]], rsem.at[k_g[0] + r], device_id=g_dst[n], device_id_type=MESH)
        lp = pltpu.make_async_copy(src, gl.at[0], lsem.at[2])

        @pl.when(jnp.logical_not(here))
        def _(cp=cp):
            cp.start()

        @pl.when(here)
        def _(lp=lp):
            lp.start()
        g_sends.append((here, cp, lp))

    w_copy.wait()

    @pl.loop(0, 6)
    def _(i):
        rows = pl.ds(pl.multiple_of(i * 256, 256), 256)
        wt[:, rows] = wv[rows, :].T

    x_copy.wait()

    def pass_y(d):
        z = zof(d)
        arrived(xt.at[3, z, c], k_y[0][d])
        send(xt.at[3, z, c, pl.ds(0, 96)], xt.at[2, z, c, pl.ds(0, 96)], on_y(1), k_f[0][d])
        send(xt.at[3, z, c], xt.at[3, z, c], core, k_cy[0][d])
        arrived(xt.at[1, z, c], k_y[1][d])
        send(xt.at[1, z, c, pl.ds(96, 96)], xt.at[2, z, c, pl.ds(96, 96)], on_y(3), k_f[1][d])
        send(xt.at[1, z, c], xt.at[1, z, c], core, k_cy[1][d])

    pass_y(0)
    for d in (1, 3, 2):
        z = zof(d)
        arrived(xt.at[0, z, c], k_z[d])
        send(xt.at[0, z, c], xt.at[3, z, c], on_y(1), k_y[0][d])
        send(xt.at[0, z, c], xt.at[1, z, c], on_y(3), k_y[1][d])
        send(xt.at[0, z, c], xt.at[0, z, c], core, k_c0[d])

    def term(r):
        block = xt[r].reshape(1536, 384)

        @pl.loop(0, 4)
        def _(i):
            rows = pl.ds(pl.multiple_of(i * 192, 192), 192)
            pp[r, i] = jnp.dot(wt[rows, :], block, preferred_element_type=F32).astype(BF16).reshape(2, 96, 384)

    k_rz = [slot() for _ in range(4)]
    k_rx = [[None] + [slot() for _ in range(3)] for _ in range(4)]
    k_pz = [slot() for _ in range(4)]
    k_px = [[None] + [slot() for _ in range(3)] for _ in range(4)]
    k_rc = [slot() for _ in range(4)]
    k_ry = [None] + [[slot() for _ in range(4)] for _ in range(3)]
    k_rzz = [None] + [slot() for _ in range(3)]

    def step_a(r):
        term(r)
        send(pp.at[r, :, 1 - zl], rz.at[r], zlp, k_rz[r])

    def step_b(r):
        arrived(rz.at[r], k_rz[r])
        s1[r] = (pp[r, :, zl].astype(F32) + rz[r].astype(F32)).astype(BF16)
        for d in (2, 1, 3):
            send(s1.at[r, (x + d) % 4], rx.at[r, d - 1], on_x(d), k_rx[r][d])

    def step_c(r):
        total = s1[r, x].astype(F32)
        for d in (1, 3, 2):
            arrived(rx.at[r, d - 1], k_rx[r][d])
            total = total + rx[r, d - 1].astype(F32)
        pt[r, x, zl] = gelu_slope(total, gl[r].astype(F32)).astype(BF16)
        send(pt.at[r, x, zl], pt.at[r, x, zl], zlp, k_pz[r])

    def step_d(r):
        arrived(pt.at[r, x, 1 - zl], k_pz[r])
        for d in (2, 1, 3):
            send(pt.at[r, x], pt.at[r, x], on_x(d), k_px[r][d])

    def step_e(r):
        for d in (1, 3, 2):
            arrived(pt.at[r, (x - d + 4) % 4], k_px[r][d])
        block = pt[r].reshape(768, 384)

        @pl.loop(0, 4)
        def _(i):
            rows = pl.ds(pl.multiple_of(i * 384, 384), 384)
            dx[r, i] = jnp.dot(wv[rows, :], block, preferred_element_type=F32).astype(BF16).reshape(2, 192, 384)
        send(dx.at[r, :, 1 - c], rc.at[r], core, k_rc[r])

    def step_f(r):
        arrived(rc.at[r], k_rc[r])
        sy[r] = (dx[r, :, c].astype(F32) + rc[r].astype(F32)).astype(BF16)
        if r:
            for d in (2, 1, 3, 0):
                z = (zh + d) % 4
                send(sy.at[r, z], ry.at[r - 1, z], on_y(r), k_ry[r][d])

    def core_wait(r):
        if r == 0:
            for d in (0, 1, 3, 2):
                arrived(xt.at[0, zof(d), 1 - c], k_c0[d])
        elif r == 2:
            for d in (0, 1, 3, 2):
                arrived(xt.at[2, zof(d), 1 - c, pl.ds(0, 96)], k_cf[0][d])
                arrived(xt.at[2, zof(d), 1 - c, pl.ds(96, 96)], k_cf[1][d])
        else:
            for d in (0, 1, 3, 2):
                arrived(xt.at[r, zof(d), 1 - c], k_cy[0 if r == 3 else 1][d])

    core_wait(0)
    step_a(0)
    for d in (1, 3, 2):
        pass_y(d)
    step_b(0)
    core_wait(3)
    step_a(3)
    core_wait(1)
    step_a(1)
    for n in range(4):
        here, cp, lp = g_sends[n]

        @pl.when(here)
        def _(lp=lp):
            lp.wait()

    for r in range(4):
        if r == 0:
            @pl.when(jnp.logical_not(own_g))
            def _():
                arrived(gl.at[0], k_g[0])
        else:
            arrived(gl.at[r], k_g[r])
    step_c(0)
    for d in (0, 1, 3, 2):
        z = zof(d)
        for half in range(2):
            part = xt.at[2, z, c, pl.ds(half * 96, 96)]
            arrived(part, k_f[half][d])
            send(part, part, core, k_cf[half][d])
    step_b(3)
    step_b(1)
    core_wait(2)
    step_a(2)
    step_c(3)
    step_d(0)
    step_c(1)
    step_b(2)
    step_d(3)
    step_d(1)
    step_c(2)
    step_d(2)
    step_e(3)
    step_e(1)
    step_f(3)
    step_f(1)
    step_e(2)
    step_e(0)
    step_f(2)
    step_f(0)

    @pl.loop(0, 4)
    def _(i):
        total = None
        for r in range(4):
            one = lax.dot_general(xt[r, i].reshape(384, 384), pt[r].reshape(768, 384), (((1,), (1,)), ((), ())),
                                  preferred_element_type=F32)
            total = one if total is None else total + one
        dwv[pl.ds(pl.multiple_of(i * 384, 384), 384), :] = total.astype(BF16)
    dw_copy = pltpu.make_async_copy(dwv, dw_out, lsem.at[3])
    dw_copy.start()

    total = None
    for d in (2, 1, 3, 0):
        z = (zh + d) % 4
        part = sy[0, z].astype(F32)
        for r in (3, 1, 2):
            arrived(ry.at[r - 1, z], k_ry[r][d])
            part = part + ry[r - 1, z].astype(F32)
        if d:
            sz[d - 1] = part.astype(BF16)
            send(sz.at[d - 1], rzz.at[d - 1], on_z(d), k_rzz[d])
        else:
            total = part
    for d in (1, 3, 2):
        arrived(rzz.at[d - 1], k_rzz[d])
        total = total + rzz[d - 1].astype(F32)
    dx_out[...] = total.astype(BF16)

    for cp in sends:
        cp.wait_send()
    for here, cp, lp in g_sends:
        @pl.when(jnp.logical_not(here))
        def _(cp=cp):
            cp.wait_send()
    dw_copy.wait()
    assert count[0] <= N_SEM, count


def local(saved_input, weight, out_grad):
    vmem = pl.BlockSpec(memory_space=pltpu.VMEM)
    scratch = [
        (1536, 768), (768, 1536), (384, 384), (4, 96, 384),
        (4, 4, 2, 192, 384),
        (4, 4, 2, 96, 384), (4, 4, 96, 384), (4, 4, 96, 384),
        (4, 3, 96, 384), (4, 4, 2, 96, 384),
        (4, 4, 2, 192, 384), (4, 4, 192, 384), (4, 4, 192, 384),
        (3, 4, 192, 384), (3, 192, 384), (3, 192, 384),
        (1536, 768),
    ]
    dx, dw = pl.pallas_call(
        kernel,
        out_shape=[jax.ShapeDtypeStruct((192, 384), BF16), jax.ShapeDtypeStruct((1536, 768), BF16)],
        in_specs=[vmem, pl.BlockSpec(memory_space=pl.ANY), vmem],
        out_specs=[vmem, pl.BlockSpec(memory_space=pl.ANY)],
        scratch_shapes=[pltpu.VMEM(s, BF16) for s in scratch] + [
            pltpu.SemaphoreType.DMA((N_SEM,)), pltpu.SemaphoreType.DMA((N_SEM,)), pltpu.SemaphoreType.DMA((4,))],
        compiler_params=pltpu.CompilerParams(collective_id=0, has_side_effects=True, vmem_limit_bytes=56 * 2**20),
        cost_estimate=pl.CostEstimate(flops=3 * 2 * 1536 * 1536 * 768, bytes_accessed=8 * 2**20, transcendentals=0),
        name="fused_layer",
    )(saved_input.T, weight, out_grad)
    return dx.T, dw


def solution(mesh):
    placed = (P("gx", ("gy", "gz")), P("gy", ("gz", "gx")), P("gx", ("gz", "gy")))
    return jax.shard_map(
        local,
        mesh=mesh,
        in_specs=placed,
        out_specs=(P("gx", ("gy", "gz")), P("gy", ("gz", "gx"))),
        check_vma=False,
    )
```

time: 326 us -> 133 us (0.41)
  waiting for transfers between devices: 262 us -> 0 us
  Pallas kernels: 0 us -> 127 us
  matrix products: 21.6 us -> 0 us
  local copies, waits for them, and re-layouts: 22.7 us -> 4.81 us
  between operations: 14.2 us -> 0.64 us
    all_gather x3 -> x0, waiting for transfers between devices: 135 us -> none  [the longest x1 55.4 us: local(): inputs = lax.all_gather(feats, 'gx', axis=0, tiled=True)]
    pallas_call x0 -> x1, Pallas kernels: none -> 127 us  [local(): pl.pallas_call(kernel, out_shape=[jax.ShapeDtypeStruct((192, 384), BF16),...]
    reduce_scatter x2 -> x0, waiting for transfers between devices: 101 us -> none  [the longest x1 57.4 us: local(): lax.psum_scatter(input_terms, 'gx', scatter_dimension=0, tiled=True)]
    unnamed x7 -> x0, waiting for transfers between devices: 26.2 us -> none
    dot_general x3 -> x0, matrix products: 21.6 us -> none  [the longest x1 8.36 us: local(): lax.dot_general(inputs, pre_grad, (((0,), (0,)), ((), ())), preferred_ele...]
    reshape x2 -> x0, local copies, waits for them, and re-layouts: 9.86 us -> none  [the longest x1 5.77 us: local(): partial_value.reshape(4, 384, 2, 384).transpose(0, 2, 1, 3)]
    unnamed x9 -> x2, local copies, waits for them, and re-layouts: 9.48 us -> 4.81 us
    transpose x1 -> x0, local copies, waits for them, and re-layouts: 3.39 us -> none  [local(): partial_value.reshape(4, 384, 2, 384).transpose(0, 2, 1, 3)]
  transfers between devices with their start and end apart: 7 -> 0, of which waited for: 6 -> 0; matrix products, arithmetic and copies ran while one was open for 4% -> 0% of each run, Pallas kernels for 0% -> 0%
where the time goes in v2:
time: 133 us; the launch traced here: 132 us
  Pallas kernels  127 us (95%)
  local copies, waits for them, and re-layouts  4.81 us (4%)
    pallas_call x1, Pallas kernels, local(): pl.pallas_call(kernel, out_shape=[jax.ShapeDtypeStruct((192, 384), BF16),...  127 us
    unnamed x2, local copies, waits for them, and re-layouts  4.81 us

profile of v2, /device:TPU:1, one launch (start us, length us, event | category | flops | bytes accessed | tf_op | source)
XLA Modules:
  0.0 132.3 jit_solution(10427294764498050291)
XLA Ops:
  0.6 126.8 %fused_layer.1 = (bf16[192,384]{1,0:T(8,128)(2,1)}, bf16[1536,768]{1,0:T(8,128)(2,1)}) custom-call(bf16[192,384]{1,0:T(8,128)(2,1)} %bitcast.3, bf16[1536,768]{1,0:T(8,128)(2,1)} %w_hbm.1, bf16[384,384]{1,0:T(8,128)(2,1)} %g_ref.1), custom_call_target="tpu_custom_call" | custom-call | flops 10871635968 | bytes 8388608 | tf_op jit(solution)/shard_map/fused_layer/pallas_call | solution.py:308
  127.5 1.6 %copy.7 = bf16[384,192]{0,1:T(8,128)(2,1)} copy(bf16[384,192]{0,1:T(8,128)(2,1)} %bitcast.2) | data formatting | bytes 294912
  129.1 3.2 %copy.8 = bf16[1536,768]{1,0:T(8,128)(2,1)} copy(bf16[1536,768]{1,0:T(8,128)(2,1)} %get-tuple-element.9) | data formatting | bytes 4718592

commit v3 on v0

v3 whole, which is shorter than its diff:
```python
import functools

import jax
import jax.numpy as jnp
from jax import lax
from jax.experimental import pallas as pl
from jax.experimental.pallas import tpu as pltpu
from jax.sharding import PartitionSpec as P

MESH = pl.DeviceIdType.MESH
F32 = jnp.float32
BF16 = jnp.bfloat16
ROOT = 0.7978845608028654
CUBE = 0.044715
N_RECV = 89
N_SEND = 56

PARTS = ((0, 128), (128, 256))
ORDER = (
    "P", "W", "Y00", "Z30", "Y01", "Z10", "Y30", "Z11", "Z20", "Z31", "Y10", "K00", "A00", "Y20", "Y11", "Z21",
    "G", "H01", "K10", "A10", "H00", "H20", "K01", "H30", "A01", "H10", "K30", "H11", "Y31", "A30", "B00", "Y21",
    "K20", "A20", "B10", "K31", "A31", "B20", "K11", "B30", "A11", "H31", "H21", "C10", "K21", "A21", "C20",
    "D10", "C30", "B11", "C00", "D20", "V10", "B01", "B21", "V20", "E10", "D30", "C11", "B31", "E20", "V30",
    "C21", "D21", "F20", "D00", "C01", "E30", "D11", "C31", "V00", "F10", "F30", "V21", "E21", "D31", "E00",
    "F21", "V31", "V11", "F00", "S20", "S30", "D01", "E11", "E31", "F11", "F31", "S10", "V01", "E01", "F01",
    "S21", "M0", "S11", "S00", "S31", "T0", "S01", "M1", "T1",
)
SUM = "dxzxdzzz"
GATHER = "tssstdtd"


def gelu_slope(pre, grad):
    square = pre * pre
    tanh = jnp.tanh(ROOT * (pre + CUBE * (pre * square)))
    slope = 0.5 * (1.0 + tanh) + (0.5 * ROOT) * pre * (1.0 - tanh * tanh) * (1.0 + 3.0 * CUBE * square)
    return grad * slope


def part_scratch(n):
    return dict(
        xt=(4, 4, 2, 192, n),
        pp=(4, 4, 2, 96, n),
        rz=(4, 4, 96, n), s1=(4, 4, 96, n), rx=(4, 3, 96, n),
        rx2=(4, 3, 2, 96, n), s2=(4, 2, 96, n), rz2=(4, 96, n), rw=(4, 2, 96, n), sw=(4, 2, 2, 96, n),
        rd=(4, 7, 96, n),
        pt=(4, 4, 2, 96, n),
        dx=(4, 4, 2, 192, n),
        rc=(4, 4, 192, n), sy=(4, 4, 192, n), ry=(2, 4, 192, n), rf=(2, 4, 96, n),
        sz=(4, 192, n), rzz=(4, 192, n),
    )


def kernel(order, sums, gathers, parts, x_hbm, w_hbm, g_hbm, dx_out, dw_out, gv, wv, wt, gt, gl, dwv, *refs):
    ssem, rsem, lsem, near = refs[-4:]
    names = list(part_scratch(0))
    at = [dict(zip(names, refs[p * len(names):])) for p in range(len(parts))]
    xt, pp, rz, s1, rx, rx2, s2, rz2, rw, sw, rd, pt, dx, rc, sy, ry, rf, sz, rzz = ([a[n] for a in at] for n in names)

    y, gy, gz = lax.axis_index("gx"), lax.axis_index("gy"), lax.axis_index("gz")
    zl, x = gy // 4, gy % 4
    zh, c = gz // 2, gz % 2

    core = (y, gy, zh * 2 + (1 - c))
    zlp = (y, (1 - zl) * 4 + x, gz)

    def on_y(d):
        return ((y + d) % 4, gy, gz)

    def on_x(d, e=0):
        return (y, ((zl + e) % 2) * 4 + (x + d) % 4, gz)

    def on_z(d):
        return (y, gy, ((zh + d) % 4) * 2 + c)

    def zof(d):
        return (zh - d + 4) % 4

    def xof(d):
        return (x - d + 4) % 4

    g_dst = [(2 * zl + x // 2, z * 4 + 2 * (x % 2) + k, gz) for k in range(2) for z in range(2)]
    g_rows = [(2 * k + z) * 96 for k in range(2) for z in range(2)]
    own_g = jnp.logical_and(zl == y // 2, x == 2 * (y % 2) + x // 2)

    keys, sends, pending, state = {}, [], {}, {}
    others = ((2, 1), (2, 0), (1, 1), (1, 0), (3, 1), (3, 0), (0, 1))

    def mode(table, r, p):
        return table[r * len(parts) + p]

    def slot(*key):
        return keys.setdefault(key, len(keys))

    def send_slot():
        if len(sends) >= N_SEND:
            sends[-N_SEND]()
        return ssem.at[len(sends) % N_SEND]

    def send(src, dst, to, *key):
        cp = pltpu.make_async_remote_copy(src, dst, send_slot(), rsem.at[slot(*key)], device_id=to, device_id_type=MESH)
        cp.start()
        sends.append(cp.wait_send)
        pending.setdefault(key, []).append(dst)

    def arrived(ref, *key):
        assert ref.size == sum(dst.size for dst in pending.pop(key))
        k = slot(*key)
        pltpu.make_async_remote_copy(ref, ref, ssem.at[0], rsem.at[k], device_id=core, device_id_type=MESH).wait_recv()

    barrier = pltpu.get_barrier_semaphore()
    partners = [core, zlp] + [on_y(d) for d in (1, 2, 3)] + [on_x(d) for d in (1, 2, 3)] + [on_z(d) for d in (1, 3)]
    for to in partners:
        pl.semaphore_signal(barrier, inc=1, device_id=to, device_id_type=MESH)
    x_copies = [pltpu.make_async_copy(x_hbm.at[:, pl.ds(t, n)], xt[p].at[0, zh, c], lsem.at[5 + p])
                for p, (t, n) in enumerate(parts)]
    g_copy = pltpu.make_async_copy(g_hbm, gv, lsem.at[4])
    w_copy = pltpu.make_async_copy(w_hbm, wv, lsem.at[0])
    for cp in x_copies + [g_copy, w_copy]:
        cp.start()

    pl.semaphore_wait(barrier, len(partners))
    for d in (1, 2, 3):
        pl.semaphore_signal(near.at[0], inc=1, device_id=on_x(d), device_id_type=MESH)

    halves = {1: pl.ds(0, 96), 3: pl.ds(96, 96)}

    def step_p():
        for p in range(len(parts)):
            x_copies[p].wait()
            own = xt[p].at[0, zh, c]
            send(own, own, on_z(1), "z", 1, p)
            send(own, own, on_z(3), "z", 3, p)
            send(own, xt[p].at[3, zh, c], on_y(1), "y", 3, 0, p)
            send(own, xt[p].at[1, zh, c], on_y(3), "y", 1, 0, p)
            send(own, own, core, "k", 0, p)

    def step_w():
        g_copy.wait()
        gt[...] = gv[...].T
        w_copy.wait()

        @pl.loop(0, 2)
        def _(i):
            rows = pl.ds(pl.multiple_of(i * 768, 768), 768)
            wt[:, rows] = wv[rows, :].T
        pl.semaphore_wait(near.at[0], 3)
        for d in (1, 2, 3):
            pl.semaphore_signal(near.at[1], inc=1, device_id=on_y(d), device_id_type=MESH)

    def step_g():
        pl.semaphore_wait(near.at[1], 3)
        state["g"] = []
        for n in range(4):
            a, dgy, _ = g_dst[n]
            r = (y - a + 4) % 4
            here = jnp.logical_and(a == y, dgy == gy)
            src = gt.at[pl.ds(g_rows[n], 96)]
            cp = pltpu.make_async_remote_copy(src, gl.at[r], send_slot(), rsem.at[slot("g")], device_id=g_dst[n], device_id_type=MESH)
            lp = pltpu.make_async_copy(src, gl.at[0], lsem.at[2])

            @pl.when(jnp.logical_not(here))
            def _(cp=cp):
                cp.start()

            @pl.when(here)
            def _(lp=lp):
                lp.start()

            def sent(here=here, cp=cp):
                @pl.when(jnp.logical_not(here))
                def _():
                    cp.wait_send()
            sends.append(sent)
            state["g"].append((here, lp))

    def g_wait():
        if "g" not in state:
            return
        for here, lp in state.pop("g"):
            @pl.when(here)
            def _(lp=lp):
                lp.wait()
        k = slot("g")

        @pl.when(own_g)
        def _():
            part = gl.at[pl.ds(1, 3)]
            pltpu.make_async_remote_copy(part, part, ssem.at[0], rsem.at[k], device_id=core, device_id_type=MESH).wait_recv()

        @pl.when(jnp.logical_not(own_g))
        def _():
            pltpu.make_async_remote_copy(gl, gl, ssem.at[0], rsem.at[k], device_id=core, device_id_type=MESH).wait_recv()

    def step_z(d, p):
        shard = (zof(d), c)
        here = xt[p].at[(0,) + shard]
        if d == 2:
            arrived(here, "zf", p)
        else:
            arrived(here, "z", d, p)
            half = xt[p].at[(0,) + shard + (halves[d],)]
            send(half, half, on_z(d), "zf", p)
        send(here, xt[p].at[(3,) + shard], on_y(1), "y", 3, d, p)
        send(here, xt[p].at[(1,) + shard], on_y(3), "y", 1, d, p)
        send(here, here, core, "k", 0, p)

    def step_y(d, p):
        shard = (zof(d), c)
        for r, to in ((3, 1), (1, 3)):
            here = xt[p].at[(r,) + shard]
            arrived(here, "y", r, d, p)
            send(xt[p].at[(r,) + shard + (halves[to],)], xt[p].at[(2,) + shard + (halves[to],)], on_y(to), "f", d, p)
            send(here, here, core, "k", r, p)

    def step_h(d, p):
        shard = (zof(d), c)
        here = xt[p].at[(2,) + shard]
        arrived(here, "f", d, p)
        send(here, here, core, "k", 2, p)

    def step_k(r, p):
        arrived(xt[p].at[r, :, 1 - c], "k", r, p)

    def step_a(r, p):
        n = parts[p][1]
        term = jnp.dot(wt[...], xt[p][r].reshape(1536, n), preferred_element_type=F32)
        pp[p][r] = term.astype(BF16).reshape(4, 2, 96, n)
        m = mode(sums, r, p)
        if m == "x":
            for d in (2, 1, 3):
                send(pp[p].at[r, (x + d) % 4], rx2[p].at[r, d - 1], on_x(d), "sx", r, p)
        elif m == "w":
            for k, d in enumerate((1, 3)):
                send(pp[p].at[r, (x + 2) % 4, k], rw[p].at[r, k], on_x(d), "sw", r, p)
        elif m == "z":
            send(pp[p].at[r, :, 1 - zl], rz[p].at[r], zlp, "sz", r, p)
        else:
            for i, (d, e) in enumerate(others):
                send(pp[p].at[r, (x + d) % 4, (zl + e) % 2], rd[p].at[r, i], on_x(d, e), "sd", r, p)

    def step_j(r, p):
        if mode(sums, r, p) == "w":
            arrived(rw[p].at[r], "sw", r, p)
            for k, d in enumerate((1, 3)):
                sw[p][r, k, k] = (pp[p][r, (x + d) % 4, k].astype(F32) + rw[p][r, k].astype(F32)).astype(BF16)
                sw[p][r, k, 1 - k] = pp[p][r, (x + d) % 4, 1 - k]
                send(sw[p].at[r, k], rx2[p].at[r, k], on_x(d), "sx", r, p)

    def step_b(r, p):
        m = mode(sums, r, p)
        if m in "xw":
            total = pp[p][r, x].astype(F32)
            came = 3 if m == "x" else 2
            arrived(rx2[p].at[r, pl.ds(0, came)], "sx", r, p)
            for i in range(came):
                total = total + rx2[p][r, i].astype(F32)
            s2[p][r] = total.astype(BF16)
            send(s2[p].at[r, 1 - zl], rz2[p].at[r], zlp, "sz", r, p)
        elif m == "z":
            arrived(rz[p].at[r], "sz", r, p)
            s1[p][r] = (pp[p][r, :, zl].astype(F32) + rz[p][r].astype(F32)).astype(BF16)
            for d in (2, 1, 3):
                send(s1[p].at[r, (x + d) % 4], rx[p].at[r, d - 1], on_x(d), "sx", r, p)

    def step_c(r, p):
        g_wait()
        m = mode(sums, r, p)
        if m in "xw":
            arrived(rz2[p].at[r], "sz", r, p)
            total = s2[p][r, zl].astype(F32) + rz2[p][r].astype(F32)
        elif m == "z":
            total = s1[p][r, x].astype(F32)
            arrived(rx[p].at[r], "sx", r, p)
            for i in range(3):
                total = total + rx[p][r, i].astype(F32)
        else:
            total = pp[p][r, x, zl].astype(F32)
            arrived(rd[p].at[r], "sd", r, p)
            for i in range(7):
                total = total + rd[p][r, i].astype(F32)
        t, n = parts[p]
        pt[p][r, x, zl] = gelu_slope(total, gl[r, :, t:t + n].astype(F32)).astype(BF16)
        own = pt[p].at[r, x, zl]
        if mode(gathers, r, p) == "d":
            for d, e in others:
                send(own, own, on_x(d, e), "pd", r, p)
        elif mode(gathers, r, p) == "t":
            for d in (2, 1, 3):
                send(own, own, on_x(d), "px", r, p, 0)
        else:
            send(own, own, zlp, "pz", r, p)

    def step_d(r, p):
        m = mode(gathers, r, p)
        if m == "t":
            arrived(rx[p].at[r], "px", r, p, 0)
            send(pt[p].at[r, :, zl], pt[p].at[r, :, zl], zlp, "pz", r, p)
        elif m != "d":
            arrived(pt[p].at[r, x, 1 - zl], "pz", r, p)
            for d in (1, 3) if m == "r" else (2, 1, 3):
                send(pt[p].at[r, x], pt[p].at[r, x], on_x(d), "px", r, p, d if m == "r" else 0)

    def step_v(r, p):
        if mode(gathers, r, p) == "r":
            for d in (1, 3):
                arrived(pt[p].at[r, xof(d)], "px", r, p, d)
                send(pt[p].at[r, xof(d), d // 2], pt[p].at[r, xof(d), d // 2], on_x(d), "pf", r, p)

    def step_e(r, p):
        m = mode(gathers, r, p)
        if m == "r":
            arrived(pt[p].at[r, xof(2)], "pf", r, p)
        elif m == "t":
            arrived(pt[p].at[r, :, 1 - zl], "pz", r, p)
        elif m == "s":
            arrived(rx2[p].at[r], "px", r, p, 0)
        else:
            arrived(rd[p].at[r], "pd", r, p)
        n = parts[p][1]
        for d in (2, 1, 3, 0):
            z = (zh + d) % 4
            rows = pl.ds(pl.multiple_of(z * 384, 384), 384)
            term = jnp.dot(wv[rows, :], pt[p][r].reshape(768, n), preferred_element_type=F32)
            dx[p][r, z] = term.astype(BF16).reshape(2, 192, n)
            send(dx[p].at[r, z, 1 - c], rc[p].at[r, z], core, "dc", r, p)

    def step_f(r, p):
        arrived(rc[p].at[r], "dc", r, p)
        if r % 2:
            arrived(rf[p].at[r // 2], "yf", r, p)
        for d in (2, 1, 3, 0):
            z = (zh + d) % 4
            total = dx[p][r, z, c].astype(F32) + rc[p][r, z].astype(F32)
            if r % 2:
                lo, hi = total[:96], total[96:]
                more = rf[p][r // 2, z].astype(F32)
                sy[p][r, z, halves[r]] = ((lo if r == 1 else hi) + more).astype(BF16)
                sy[p][r, z, halves[4 - r]] = (hi if r == 1 else lo).astype(BF16)
                send(sy[p].at[r, z], ry[p].at[r // 2, z], on_y(r), "dy", p, d)
            else:
                sy[p][r, z] = total.astype(BF16)
            if r == 2:
                for k in (1, 3):
                    send(sy[p].at[r, z, halves[k]], rf[p].at[k // 2, z], on_y(k), "yf", k, p)

    def step_m(i):
        total = None
        for r in range(4):
            for p, (_, n) in enumerate(parts):
                one = lax.dot_general(xt[p][r, 2 * i:2 * i + 2].reshape(768, n), pt[p][r].reshape(768, n), (((1,), (1,)), ((), ())),
                                      preferred_element_type=F32)
                total = one if total is None else total + one
        rows = pl.ds(i * 768, 768)
        dwv[rows, :] = total.astype(BF16)
        state["dw", i] = pltpu.make_async_copy(dwv.at[rows], dw_out.at[rows], lsem.at[1 if i else 3])
        state["dw", i].start()

    def step_s(d, p):
        z = (zh + d) % 4
        part = sy[p][0, z].astype(F32)
        arrived(ry[p].at[:, z], "dy", p, d)
        for k in range(2):
            part = part + ry[p][k, z].astype(F32)
        if d:
            sz[p][d] = part.astype(BF16)
            send(sz[p].at[d], rzz[p].at[d], on_z(d), "dz", p)
        else:
            state["own", p] = part

    def step_t(p):
        total = state["own", p]
        arrived(rzz[p].at[pl.ds(1, 3)], "dz", p)
        for d in (1, 2, 3):
            total = total + rzz[p][d].astype(F32)
        t, n = parts[p]
        dx_out[:, t:t + n] = total.astype(BF16)

    steps = dict(P=step_p, W=step_w, G=step_g, Z=step_z, Y=step_y, H=step_h, K=step_k, A=step_a, J=step_j, B=step_b, C=step_c,
                 D=step_d, V=step_v, E=step_e, F=step_f, M=step_m, S=step_s, T=step_t)
    for name in order:
        steps[name[0]](*map(int, name[1:]))

    for sent in sends[-N_SEND:]:
        sent()
    for i in range(2):
        state["dw", i].wait()
    assert not pending and len(keys) <= N_RECV, len(keys)


def copy_kernel(dx_in, dw_in, dx_out, dw_out, dx, dw, sems):
    spans = [(dw_in, dw, dw_out, pl.ds(i * 384, 384)) for i in range(4)] + [(dx_in, dx, dx_out, pl.ds(0, 192))]
    ins = [pltpu.make_async_copy(a.at[rows], b.at[rows], sems.at[0, i]) for i, (a, b, _, rows) in enumerate(spans)]
    outs = [pltpu.make_async_copy(b.at[rows], o.at[rows], sems.at[1, i]) for i, (_, b, o, rows) in enumerate(spans)]
    for cp in ins:
        cp.start()
    for cp, out in zip(ins, outs):
        cp.wait()
        out.start()
    for out in outs:
        out.wait()


SCRATCH = [(384, 384), (1536, 768), (768, 1536), (384, 384), (4, 96, 384), (1536, 768)]


def local(saved_input, weight, out_grad, order=ORDER, sums=SUM, gathers=GATHER, parts=PARTS, cid=0, name="fused_layer"):
    vmem = pl.BlockSpec(memory_space=pltpu.VMEM)
    shapes = SCRATCH + [s for _, n in parts for s in part_scratch(n).values()]
    dx, dw = pl.pallas_call(
        functools.partial(kernel, order, sums, gathers, parts),
        out_shape=[jax.ShapeDtypeStruct((192, 384), BF16), jax.ShapeDtypeStruct((1536, 768), BF16)],
        in_specs=[pl.BlockSpec(memory_space=pl.ANY)] * 3,
        out_specs=[vmem, pl.BlockSpec(memory_space=pl.ANY)],
        scratch_shapes=[pltpu.VMEM(s, BF16) for s in shapes] + [
            pltpu.SemaphoreType.DMA((N_SEND,)), pltpu.SemaphoreType.DMA((N_RECV,)), pltpu.SemaphoreType.DMA((8,)), pltpu.SemaphoreType.REGULAR((2,))],
        compiler_params=pltpu.CompilerParams(collective_id=cid, has_side_effects=True, vmem_limit_bytes=60 * 2**20),
        cost_estimate=pl.CostEstimate(flops=3 * 2 * 1536 * 1536 * 768, bytes_accessed=8 * 2**20, transcendentals=0),
        name=name,
    )(saved_input.T, weight, out_grad)
    hbm = pl.BlockSpec(memory_space=pl.ANY)
    dx, dw = pl.pallas_call(
        copy_kernel,
        out_shape=[jax.ShapeDtypeStruct((192, 384), BF16), jax.ShapeDtypeStruct((1536, 768), BF16)],
        in_specs=[hbm] * 2,
        out_specs=[hbm] * 2,
        scratch_shapes=[pltpu.VMEM((192, 384), BF16), pltpu.VMEM((1536, 768), BF16), pltpu.SemaphoreType.DMA((2, 5))],
        name="results",
    )(dx, dw)
    return dx.T, dw


def solution(mesh):
    placed = (P("gx", ("gy", "gz")), P("gy", ("gz", "gx")), P("gx", ("gz", "gy")))
    return jax.shard_map(
        local,
        mesh=mesh,
        in_specs=placed,
        out_specs=(P("gx", ("gy", "gz")), P("gy", ("gz", "gx"))),
        check_vma=False,
    )
```

time: 432 us -> 93.8 us (0.22)
  waiting for transfers between devices: 379 us -> 0 us
  Pallas kernels: 0 us -> 92.9 us
  matrix products: 32.3 us -> 0 us
  between operations: 14.1 us -> 0.8 us
  local copies, waits for them, and re-layouts: 5.68 us -> 0 us
    all_gather x3 -> x0, waiting for transfers between devices: 164 us -> none  [the longest x1 94.8 us: local(): weights_whole = lax.all_gather(weight, 'gx', axis=1, tiled=True)]
    reduce_scatter x2 -> x0, waiting for transfers between devices: 119 us -> none  [the longest x1 82.7 us: local(): lax.psum_scatter(weight_terms.astype(jnp.bfloat16), 'gx', scatter_dimensi...]
    psum x1 -> x0, waiting for transfers between devices: 93.1 us -> none  [local(): pre = lax.psum(partial_value.astype(jnp.bfloat16), 'gy').astype(jnp.float32)]
    pallas_call x0 -> x2, Pallas kernels: none -> 92.9 us  [the longest x1 90.3 us: local(): pl.pallas_call(functools.partial(kernel, order, sums, gathers, parts), ou...]
    dot_general x3 -> x0, matrix products: 32.3 us -> none  [the longest x1 12 us: local(): lax.dot_general(inputs_whole, pre_grad, (((0,), (0,)), ((), ())), preferr...]
    unnamed x5 -> x0, local copies, waits for them, and re-layouts: 5.68 us -> none
  transfers between devices with their start and end apart: 6 -> 0, of which waited for: 6 -> 0; matrix products, arithmetic and copies ran while one was open for 6% -> 0% of each run, Pallas kernels for 0% -> 0%
where the time goes in v3:
time: 93.8 us; the launch traced here: 93.7 us
  Pallas kernels  92.9 us (99%)
    pallas_call x1, Pallas kernels, local(): pl.pallas_call(functools.partial(kernel, order, sums, gathers, parts), ou...  90.3 us
    pallas_call x1, Pallas kernels, local(): pl.pallas_call(copy_kernel, out_shape=[jax.ShapeDtypeStruct((192, 384), B...  2.59 us

profile of v3, /device:TPU:1, one launch (start us, length us, event | category | flops | bytes accessed | tf_op | source)
XLA Modules:
  0.0 93.7 jit_solution(13695330012692635959)
XLA Ops:
  0.6 90.3 %fused_layer.1 = (bf16[192,384]{1,0:T(8,128)(2,1)}, bf16[1536,768]{1,0:T(8,128)(2,1)}) custom-call(bf16[192,384]{1,0:T(8,128)(2,1)} %bitcast.2, bf16[1536,768]{1,0:T(8,128)(2,1)} %w_hbm.1, bf16[384,384]{1,0:T(8,128)(2,1)} %g_hbm.1), custom_call_target="tpu_custom_call" | custom-call | flops 10871635968 | bytes 8388608 | tf_op jit(solution)/shard_map/fused_layer/pallas_call | solution.py:409
  90.9 2.6 %results.1 = (bf16[192,384]{1,0:T(8,128)(2,1)}, bf16[1536,768]{1,0:T(8,128)(2,1)}) custom-call(bf16[192,384]{1,0:T(8,128)(2,1)} %get-tuple-element.6.dx_in, bf16[1536,768]{1,0:T(8,128)(2,1)} %get-tuple-element.7.dw_in), custom_call_target="tpu_custom_call" | custom-call | tf_op jit(solution)/shard_map/results/pallas_call | solution.py:421

commit v4 on v3

--- a/solution.py
+++ b/solution.py
@@ -13,7 +13,7 @@
 ROOT = 0.7978845608028654
 CUBE = 0.044715
 N_RECV = 89
-N_SEND = 56
+N_SEND = 40
 
 PARTS = ((0, 128), (128, 256))
 ORDER = (
@@ -23,7 +23,7 @@
     "D10", "C30", "B11", "C00", "D20", "V10", "B01", "B21", "V20", "E10", "D30", "C11", "B31", "E20", "V30",
     "C21", "D21", "F20", "D00", "C01", "E30", "D11", "C31", "V00", "F10", "F30", "V21", "E21", "D31", "E00",
     "F21", "V31", "V11", "F00", "S20", "S30", "D01", "E11", "E31", "F11", "F31", "S10", "V01", "E01", "F01",
-    "S21", "M0", "S11", "S00", "S31", "T0", "S01", "M1", "T1",
+    "S21", "S11", "S31", "M0", "M1", "S00", "T0", "S01", "T1",
 )
 SUM = "dxzxdzzz"
 GATHER = "tssstdtd"
@@ -344,12 +344,10 @@
                     send(sy[p].at[r, z, halves[k]], rf[p].at[k // 2, z], on_y(k), "yf", k, p)
 
     def step_m(i):
-        total = None
-        for r in range(4):
-            for p, (_, n) in enumerate(parts):
-                one = lax.dot_general(xt[p][r, 2 * i:2 * i + 2].reshape(768, n), pt[p][r].reshape(768, n), (((1,), (1,)), ((), ())),
-                                      preferred_element_type=F32)
-                total = one if total is None else total + one
+        pieces = [(r, p, n) for r in range(4) for p, (_, n) in enumerate(parts)]
+        lhs = jnp.concatenate([xt[p][r, 2 * i:2 * i + 2].reshape(768, n) for r, p, n in pieces], axis=1)
+        rhs = jnp.concatenate([pt[p][r].reshape(768, n) for r, p, n in pieces], axis=1)
+        total = lax.dot_general(lhs, rhs, (((1,), (1,)), ((), ())), preferred_element_type=F32)
         rows = pl.ds(i * 768, 768)
         dwv[rows, :] = total.astype(BF16)
         state["dw", i] = pltpu.make_async_copy(dwv.at[rows], dw_out.at[rows], lsem.at[1 if i else 3])

time: 93.8 us -> 93.2 us (level)
  no operation moved by 1% of the time
where the time goes in v4:
time: 93.2 us; the launch traced here: 93.1 us
  Pallas kernels  92.3 us (99%)
    pallas_call x1, Pallas kernels, local(): pl.pallas_call(functools.partial(kernel, order, sums, gathers, parts), ou...  89.7 us
    pallas_call x1, Pallas kernels, local(): pl.pallas_call(copy_kernel, out_shape=[jax.ShapeDtypeStruct((192, 384), B...  2.59 us

profile of v4, /device:TPU:1, one launch (start us, length us, event | category | flops | bytes accessed | tf_op | source)
XLA Modules:
  0.0 93.1 jit_solution(15999203337063418541)
XLA Ops:
  0.6 89.7 %fused_layer.1 = (bf16[192,384]{1,0:T(8,128)(2,1)}, bf16[1536,768]{1,0:T(8,128)(2,1)}) custom-call(bf16[192,384]{1,0:T(8,128)(2,1)} %bitcast.2, bf16[1536,768]{1,0:T(8,128)(2,1)} %w_hbm.1, bf16[384,384]{1,0:T(8,128)(2,1)} %g_hbm.1), custom_call_target="tpu_custom_call" | custom-call | flops 10871635968 | bytes 8388608 | tf_op jit(solution)/shard_map/fused_layer/pallas_call | solution.py:407
  90.3 2.6 %results.1 = (bf16[192,384]{1,0:T(8,128)(2,1)}, bf16[1536,768]{1,0:T(8,128)(2,1)}) custom-call(bf16[192,384]{1,0:T(8,128)(2,1)} %get-tuple-element.6.dx_in, bf16[1536,768]{1,0:T(8,128)(2,1)} %get-tuple-element.7.dw_in), custom_call_target="tpu_custom_call" | custom-call | tf_op jit(solution)/shard_map/results/pallas_call | solution.py:419

commit v5 on v4

--- a/solution.py
+++ b/solution.py
@@ -13,7 +13,7 @@
 ROOT = 0.7978845608028654
 CUBE = 0.044715
 N_RECV = 89
-N_SEND = 40
+N_SEND = 32
 
 PARTS = ((0, 128), (128, 256))
 ORDER = (
@@ -371,7 +371,9 @@
         for d in (1, 2, 3):
             total = total + rzz[p][d].astype(F32)
         t, n = parts[p]
-        dx_out[:, t:t + n] = total.astype(BF16)
+        sz[p][0] = total.astype(BF16)
+        state["dx", p] = pltpu.make_async_copy(sz[p].at[0], dx_out.at[:, pl.ds(t, n)], lsem.at[5 + p])
+        state["dx", p].start()
 
     steps = dict(P=step_p, W=step_w, G=step_g, Z=step_z, Y=step_y, H=step_h, K=step_k, A=step_a, J=step_j, B=step_b, C=step_c,
                  D=step_d, V=step_v, E=step_e, F=step_f, M=step_m, S=step_s, T=step_t)
@@ -382,6 +384,8 @@
         sent()
     for i in range(2):
         state["dw", i].wait()
+    for p in range(len(parts)):
+        state["dx", p].wait()
     assert not pending and len(keys) <= N_RECV, len(keys)
 
 
@@ -402,13 +406,12 @@
 
 
 def local(saved_input, weight, out_grad, order=ORDER, sums=SUM, gathers=GATHER, parts=PARTS, cid=0, name="fused_layer"):
-    vmem = pl.BlockSpec(memory_space=pltpu.VMEM)
     shapes = SCRATCH + [s for _, n in parts for s in part_scratch(n).values()]
     dx, dw = pl.pallas_call(
         functools.partial(kernel, order, sums, gathers, parts),
         out_shape=[jax.ShapeDtypeStruct((192, 384), BF16), jax.ShapeDtypeStruct((1536, 768), BF16)],
         in_specs=[pl.BlockSpec(memory_space=pl.ANY)] * 3,
-        out_specs=[vmem, pl.BlockSpec(memory_space=pl.ANY)],
+        out_specs=[pl.BlockSpec(memory_space=pl.ANY)] * 2,
         scratch_shapes=[pltpu.VMEM(s, BF16) for s in shapes] + [
             pltpu.SemaphoreType.DMA((N_SEND,)), pltpu.SemaphoreType.DMA((N_RECV,)), pltpu.SemaphoreType.DMA((8,)), pltpu.SemaphoreType.REGULAR((2,))],
         compiler_params=pltpu.CompilerParams(collective_id=cid, has_side_effects=True, vmem_limit_bytes=60 * 2**20),

time: 93.2 us -> 93.5 us (level)
  no operation moved by 1% of the time
where the time goes in v5:
time: 93.5 us; the launch traced here: 93.3 us
  Pallas kernels  92.5 us (99%)
    pallas_call x1, Pallas kernels, local(): pl.pallas_call(functools.partial(kernel, order, sums, gathers, parts), ou...  90 us
    pallas_call x1, Pallas kernels, local(): pl.pallas_call(copy_kernel, out_shape=[jax.ShapeDtypeStruct((192, 384), B...  2.59 us

profile of v5, /device:TPU:1, one launch (start us, length us, event | category | flops | bytes accessed | tf_op | source)
XLA Modules:
  0.0 93.3 jit_solution(10129288575018408033)
XLA Ops:
  0.6 90.0 %fused_layer.1 = (bf16[192,384]{1,0:T(8,128)(2,1)}, bf16[1536,768]{1,0:T(8,128)(2,1)}) custom-call(bf16[192,384]{1,0:T(8,128)(2,1)} %bitcast.2, bf16[1536,768]{1,0:T(8,128)(2,1)} %w_hbm.1, bf16[384,384]{1,0:T(8,128)(2,1)} %g_hbm.1), custom_call_target="tpu_custom_call" | custom-call | flops 10871635968 | bytes 8388608 | tf_op jit(solution)/shard_map/fused_layer/pallas_call | solution.py:410
  90.6 2.6 %results.1 = (bf16[192,384]{1,0:T(8,128)(2,1)}, bf16[1536,768]{1,0:T(8,128)(2,1)}) custom-call(bf16[192,384]{1,0:T(8,128)(2,1)} %get-tuple-element.6.dx_in, bf16[1536,768]{1,0:T(8,128)(2,1)} %get-tuple-element.7.dw_in), custom_call_target="tpu_custom_call" | custom-call | tf_op jit(solution)/shard_map/results/pallas_call | solution.py:422
